TPU v7x, 32 devices: a whole 2x2x4 slice. The times are simulated.
32 devices in a mesh: row: 4 (over y, x), col: 8 (over z, core).
Axes of the slice: x: 2, y: 2, z: 4, core: 2. Of those that a mesh axis runs over, the one named last changes fastest.
Arguments:
- images: float32 [64, 3, 1024], P(('row', 'col')), may hold values from -16 to 16
- roots: int32 [2, 8], replicated, may hold values from 0 to 3, as said below
Outputs:
- kernel_tiles: float32 [2, 8, 16], P(None, 'row', 'col')
Inputs may be any that keep to these rules, and one draw needn't show every extreme that they name: `roots`: at each tile index every row group appears for exactly 8 / 4 column groups.
All inputs are finite; a program needn't handle non-finite values.
Results may differ from a plain program's by a relative error of at most 0.0001.
Values sent between devices are 32-bit elements; how exact they have to be, the bound alone decides.
No kernel may reach another device: no remote copies, remote signals or barrier semaphores. Data moves between devices by JAX's collectives and lax.ppermute only.
A program may use at most 64 MiB of HBM per device.

v0:
```python
import math
import jax
import jax.numpy as jnp
from jax import lax
from jax.sharding import PartitionSpec as P

WIDTH = 32
CH = 3
DEPTH = 4
weight_var = 2.0
bias_var = 0.1


def from_root(value, axis, source):
    kept = jnp.where(lax.axis_index(axis) == source, value, 0).astype(value.dtype)
    return lax.psum(kept, axis)


def passed_along(block, axis, distance):
    devices = range(lax.axis_size(axis))
    route = [((i - distance) % len(devices), i) for i in devices]
    return lax.ppermute(block, axis, route)


def box_sum(maps):
    positions = lax.broadcasted_iota(jnp.int32, maps.shape, maps.ndim - 1) % WIDTH
    leading = maps.shape[:-1]
    single = jnp.zeros(leading + (1,), jnp.float32)
    band = jnp.zeros(leading + (WIDTH,), jnp.float32)
    from_left = jnp.concatenate([single, maps[..., :-1]], axis=-1)
    from_right = jnp.concatenate([maps[..., 1:], single], axis=-1)
    across = (
        maps
        + jnp.where(positions > 0, from_left, 0.0)
        + jnp.where(positions < WIDTH - 1, from_right, 0.0)
    )
    from_above = jnp.concatenate([band, across[..., :-WIDTH]], axis=-1)
    from_below = jnp.concatenate([across[..., WIDTH:], band], axis=-1)
    return across + from_above + from_below


def relu_map(cross, self_a, self_b):
    scale_ab = jnp.sqrt(self_a * self_b)
    cosine = cross / scale_ab
    return (
        scale_ab
        * (jnp.sqrt(1.0 - cosine * cosine) + (math.pi - jnp.arccos(cosine)) * cosine)
        / (2.0 * math.pi)
    )


def self_maps(pictures):
    energy = jnp.sum(pictures * pictures, axis=1)
    level = weight_var / (9.0 * CH) * box_sum(energy) + bias_var
    stacked = [level]
    for depth_level in range(DEPTH - 1):
        level = weight_var / 9.0 * box_sum(0.5 * level) + bias_var
        stacked.append(level)
    return jnp.stack(stacked, axis=1)


def pair_kernel(row_pictures, col_pictures, row_selfs, col_selfs):
    cross = jnp.einsum("acp,bcp->abp", row_pictures, col_pictures, precision=lax.Precision.HIGHEST)
    level = weight_var / (9.0 * CH) * box_sum(cross) + bias_var
    for depth_level in range(DEPTH - 1):
        mapped = relu_map(level, row_selfs[:, None, depth_level], col_selfs[None, :, depth_level])
        level = weight_var / 9.0 * box_sum(mapped) + bias_var
    final = relu_map(level, row_selfs[:, None, DEPTH - 1], col_selfs[None, :, DEPTH - 1])
    return weight_var * jnp.mean(final, axis=-1) + bias_var


def unpack(payload):
    return (payload, self_maps(payload))


def local(images, roots):
    col_index = lax.axis_index("col")
    column = images
    tiles = []
    for turn_index in range(roots.shape[0]):
        root_group = roots[turn_index, col_index]
        row_load = from_root(images, "row", root_group)
        column = passed_along(column, "col", 1)
        row_pictures, row_selfs = unpack(row_load)
        col_pictures, col_selfs = unpack(column)
        tiles.append(pair_kernel(row_pictures, col_pictures, row_selfs, col_selfs))
    return jnp.stack(tiles)


def solution(mesh):
    in_specs = (P(("row", "col"), None, None), P())
    out_specs = P(None, "row", "col")
    return jax.shard_map(local, mesh=mesh, in_specs=in_specs, out_specs=out_specs, check_vma=False)
```

profile of v0, /device:TPU:0, one launch (start us, length us, event | category | flops | bytes accessed | tf_op | source)
XLA Modules:
  0.0 96.1 jit_solution(13346223398370563292)
XLA Ops:
  0.0 0.5 collective-permute-start
  0.5 0.7 copy-done.29
  1.1 0.7 constant_dynamic-slice_fusion.1
  3.2 18.0 %all-reduce.96 = (f32[2,3,1024]{2,0,1:T(2,128)S(1)}, f32[2,3,1024]{2,1,0:T(4,128)S(1)}) all-reduce(f32[2,3,1024]{2,0,1:T(2,128)S(1)} %broadcast_select_fusion, f32[2,3,1024]{2,1,0:T(4,128)S(1)} %copy_select_fusion), channel_id=1, replica_groups=mesh['row'=4,'col'=8] {'row'}, use_global_device_ids=true, to_apply=%region_4.5 | all-reduce | flops 12288 | bytes 98304 | tf_op jit(solution)/shard_map/psum | solution.py:16
  21.7 1.1 %fusion.97 = (f32[2,1023]{0,1:T(8,128)}, f32[2,1023]{0,1:T(8,128)}) fusion(f32[2,1024]{0,1:T(8,128)S(1)} %copy.90), kind=kLoop, calls=%fused_computation.157 | loop fusion | bytes 32736 | tf_op jit(solution)/shard_map/slice | solution.py:30
  22.8 1.0 %fusion.81 = (f32[2,1023]{0,1:T(8,128)}, f32[2,1023]{0,1:T(8,128)}) fusion(f32[2,1024]{0,1:T(8,128)S(1)} %copy.89), kind=kLoop, calls=%fused_computation.141 | loop fusion | bytes 32736 | tf_op jit(solution)/shard_map/slice | solution.py:30
  23.8 1.3 %copy.70 = f32[2,3,1024]{1,0,2:T(2,128)} copy(f32[2,3,1024]{2,1,0:T(4,128)S(1)} %get-tuple-element.6) | data formatting | bytes 49152 | tf_op jit(solution)/shard_map/psum | solution.py:16
  25.1 0.5 copy.86
  25.9 1.3 %copy.71 = f32[2,3,1024]{1,0,2:T(2,128)} copy(f32[2,3,1024]{2,0,1:T(2,128)S(1)} %collective-permute-done) | data formatting | bytes 49152 | tf_op jit(solution)/shard_map/ppermute | solution.py:22
  27.2 9.5 %fusion.116 = f32[1024,2,2]{2,1,0:T(2,128)} fusion(f32[2,3,1024]{1,0,2:T(2,128)} %copy.70, f32[2,3,1024]{1,0,2:T(2,128)} %copy.71), kind=kOutput, calls=%fused_computation.176 | convolution fusion | flops 147456 | bytes 65536 | tf_op jit(solution)/shard_map/acp,bcp->abp/dot_general | solution.py:63
  36.7 1.4 %copy.72 = f32[1024,2,2]{0,2,1:T(2,128)S(1)} copy(f32[1024,2,2]{2,1,0:T(2,128)} %fusion.116) | data formatting | bytes 32768 | tf_op jit(solution)/shard_map/acp,bcp->abp/dot_general | solution.py:63
  38.2 1.1 %fusion.83 = (f32[2,1023]{0,1:T(8,128)}, f32[2,1023]{0,1:T(8,128)}) fusion(f32[2,1024]{0,1:T(8,128)S(1)} %copy.61), kind=kLoop, calls=%fused_computation.143 | loop fusion | bytes 32736 | tf_op jit(solution)/shard_map/slice | solution.py:30
  39.4 0.2 collective-permute-start.1
  39.7 5.0 %collective-permute-done.1 = f32[2,3,1024]{2,0,1:T(2,128)S(1)} collective-permute-done((f32[2,3,1024]{2,0,1:T(2,128)S(1)}, f32[2,3,1024]{2,0,1:T(2,128)S(1)}, u32[]{:S(2)}, u32[]{:S(2)}) %collective-permute-start.1) | collective-permute-done | bytes 24608 | tf_op jit(solution)/shard_map/ppermute | solution.py:22
  44.9 1.3 %copy.87 = f32[2,3,1024]{1,0,2:T(2,128)} copy(f32[2,3,1024]{2,0,1:T(2,128)S(1)} %collective-permute-done.1) | data formatting | bytes 49152 | tf_op jit(solution)/shard_map/ppermute | solution.py:22
  46.2 9.0 %fusion.117 = f32[1024,2,2]{2,1,0:T(2,128)} fusion(f32[2,3,1024]{1,0,2:T(2,128)S(1)} %copy.86, f32[2,3,1024]{1,0,2:T(2,128)} %copy.87), kind=kOutput, calls=%fused_computation.177 | convolution fusion | flops 147456 | bytes 65536 | tf_op jit(solution)/shard_map/acp,bcp->abp/dot_general | solution.py:63
  55.2 1.4 %copy.88 = f32[1024,2,2]{0,2,1:T(2,128)S(1)} copy(f32[1024,2,2]{2,1,0:T(2,128)} %fusion.117) | data formatting | bytes 32768 | tf_op jit(solution)/shard_map/acp,bcp->abp/dot_general | solution.py:63
  56.8 0.9 copy-done.18
  58.2 2.4 %fusion.32 = (f32[2,1024]{0,1:T(8,128)S(1)}, f32[2,1024]{0,1:T(8,128)S(1)}, f32[2,1024]{0,1:T(8,128)S(1)}, f32[2,1024]{0,1:T(8,128)S(1)}) fusion(f32[2,1024]{0,1:T(8,128)S(1)} %copy.89, f32[2,1023]{0,1:T(8,128)S(1)} %copy-done.21, f32[2,1023]{0,1:T(8,128)S(1)} %copy-done.20, s32[1024]{0:T(1024)S(1)} %iota_and_fusion, s32[1024]{0:T(1024)S(1)} %fusion.64, ...), kind=kLoop, calls=%fused_computation.34 | loop fusion | flops 38912 | bytes 140224 | tf_op jit(solution)/shard_map/add | solution.py:33
  60.6 1.1 %fusion.80 = (f32[2,992]{0,1:T(8,128)}, f32[2,992]{0,1:T(8,128)}) fusion(f32[2,1024]{0,1:T(8,128)S(1)} %get-tuple-element.141), kind=kLoop, calls=%fused_computation.140 | loop fusion | bytes 31744 | tf_op jit(solution)/shard_map/slice | solution.py:37
  61.8 0.3 broadcast_multiply_fusion.2
  62.4 0.4 copy-done.2
  62.9 1.0 %fusion.95 = (f32[2,1023]{0,1:T(8,128)}, f32[2,1023]{0,1:T(8,128)}) fusion(f32[2,1024]{0,1:T(8,128)S(1)} %get-tuple-element.29), kind=kLoop, calls=%fused_computation.155 | loop fusion | bytes 32736 | tf_op jit(solution)/shard_map/slice | solution.py:30
  64.0 1.0 %copy-done.26 = f32[2,992]{0,1:T(8,128)S(1)} copy-done((f32[2,992]{0,1:T(8,128)S(1)}, f32[2,992]{0,1:T(8,128)}, u32[]{:S(2)}) %copy-start.26) | copy-done | bytes 7960
  65.1 1.3 %broadcast_multiply_fusion.8 = (f32[2,1024]{0,1:T(8,128)}, f32[2,1024]{0,1:T(8,128)S(1)}, f32[2,1024]{0,1:T(8,128)}, f32[2,1024]{0,1:T(8,128)S(1)}) fusion(f32[2,992]{0,1:T(8,128)S(1)} %get-tuple-element.60, f32[2,1024]{0,1:T(8,128)S(1)} %get-tuple-element.144, f32[2,992]{0,1:T(8,128)S(1)} %get-tuple-element.59, f32[2,992]{0,1:T(8,128)S(1)} %copy-done.27, ...), kind=kLoop, calls=%fused_computation.90 | loop fusion | flops 20480 | bytes 80896 | tf_op jit(solution)/shard_map/mul | solution.py:57
  66.7 0.4 copy-done.4
  67.4 0.3 multiply_multiply_fusion.5
  68.0 1.0 copy-done.9
  69.1 0.8 copy-done.25
  70.6 1.6 %fusion.33 = (f32[2,1024]{0,1:T(8,128)S(1)}, f32[2,1024]{0,1:T(8,128)S(1)}, f32[2,1024]{0,1:T(8,128)S(1)}, f32[2,1024]{0,1:T(8,128)S(1)}) fusion(f32[2,1023]{0,1:T(8,128)S(1)} %get-tuple-element.50, f32[2,1023]{0,1:T(8,128)S(1)} %get-tuple-element.49, s32[1024]{0:T(1024)S(1)} %iota_and_fusion, s32[1024]{0:T(1024)S(1)} %fusion.64, ...), kind=kLoop, calls=%fused_computation.35 | loop fusion | flops 47104 | bytes 140224 | tf_op jit(solution)/shard_map/add | solution.py:33
  72.6 1.1 %fusion.73 = (f32[2,1023]{0,1:T(8,128)}, f32[2,1023]{0,1:T(8,128)}) fusion(f32[2,1024]{0,1:T(8,128)S(1)} %get-tuple-element.11), kind=kLoop, calls=%fused_computation.133 | loop fusion | bytes 32736 | tf_op jit(solution)/shard_map/slice | solution.py:30
  74.1 1.0 %fusion.91 = (f32[2,1023]{0,1:T(8,128)}, f32[2,1023]{0,1:T(8,128)}) fusion(f32[2,1024]{0,1:T(8,128)S(1)} %get-tuple-element.25), kind=kLoop, calls=%fused_computation.151 | loop fusion | bytes 32736 | tf_op jit(solution)/shard_map/slice | solution.py:30
  75.5 1.1 %fusion.89 = (f32[2,1023]{0,1:T(8,128)}, f32[2,1023]{0,1:T(8,128)}) fusion(f32[2,1024]{0,1:T(8,128)S(1)} %get-tuple-element.23), kind=kLoop, calls=%fused_computation.149 | loop fusion | bytes 32736 | tf_op jit(solution)/shard_map/slice | solution.py:30
  77.0 0.3 multiply_multiply_fusion.4
  77.7 0.9 copy-done.16
  79.1 2.7 %fusion.34 = (f32[2,1024]{0,1:T(8,128)S(1)}, f32[2,1024]{0,1:T(8,128)S(1)}, f32[2,1024]{0,1:T(8,128)S(1)}, f32[2,1024]{0,1:T(8,128)S(1)}) fusion(f32[2,1023]{0,1:T(8,128)S(1)} %copy-done.17, f32[2,1023]{0,1:T(8,128)S(1)} %copy-done.16, s32[1024]{0:T(1024)S(1)} %iota_and_fusion, s32[1024]{0:T(1024)S(1)} %fusion.64, pred[1024]{0:T(1024)(128)(4,1)S(1)} %fusion.67, ...), kind=kLoop, calls=%fused_computation.36 | loop fusion | flops 47104 | bytes 140224 | tf_op jit(solution)/shard_map/add | solution.py:33
  82.2 1.1 %fusion.69 = (f32[2,1023]{0,1:T(8,128)}, f32[2,1023]{0,1:T(8,128)}) fusion(f32[2,1024]{0,1:T(8,128)S(1)} %get-tuple-element.7), kind=kLoop, calls=%fused_computation.129 | loop fusion | bytes 32736 | tf_op jit(solution)/shard_map/slice | solution.py:30
  83.7 1.0 %fusion.87 = (f32[2,1023]{0,1:T(8,128)}, f32[2,1023]{0,1:T(8,128)}) fusion(f32[2,1024]{0,1:T(8,128)S(1)} %get-tuple-element.21), kind=kLoop, calls=%fused_computation.147 | loop fusion | bytes 32736 | tf_op jit(solution)/shard_map/slice | solution.py:30
  85.1 1.1 %fusion.85 = (f32[2,1023]{0,1:T(8,128)}, f32[2,1023]{0,1:T(8,128)}) fusion(f32[2,1024]{0,1:T(8,128)S(1)} %get-tuple-element.19), kind=kLoop, calls=%fused_computation.145 | loop fusion | bytes 32736 | tf_op jit(solution)/shard_map/slice | solution.py:30
  86.6 0.3 multiply_multiply_fusion.3
  87.2 0.3 multiply_multiply_fusion.2
  87.8 0.3 multiply_multiply_fusion.1
  88.3 0.3 multiply_multiply_fusion
  89.0 0.9 copy-done.1
  90.4 2.8 %fusion.35 = (f32[2,1024]{0,1:T(8,128)S(1)}, f32[2,1024]{0,1:T(8,128)S(1)}, f32[2,1024]{0,1:T(8,128)S(1)}, f32[2,1024]{0,1:T(8,128)S(1)}) fusion(f32[2,1023]{0,1:T(8,128)S(1)} %copy-done.12, f32[2,1023]{0,1:T(8,128)S(1)} %copy-done.11, s32[1024]{0:T(1024)S(1)} %iota_and_fusion, s32[1024]{0:T(1024)S(1)} %fusion.64, pred[1024]{0:T(1024)(128)(4,1)S(1)} %fusion.67, ...), kind=kLoop, calls=%fused_computation.37 | loop fusion | flops 47104 | bytes 140224 | tf_op jit(solution)/shard_map/add | solution.py:33
  94.4 0.3 multiply_reduce_fusion.4
  95.2 0.3 multiply_reduce_fusion.5
  95.5 0.6 pad_maximum_fusion
  (139 shorter events, 11.5 us)
Async XLA Ops:
  0.0 3.1 %copy-start.28 = (f32[2,3,1024]{2,0,1:T(2,128)S(1)}, f32[2,3,1024]{2,0,1:T(2,128)}, u32[]{:S(2)}) copy-start(f32[2,3,1024]{2,0,1:T(2,128)} %param.2) | copy-start | bytes 73732
  0.0 25.6 %collective-permute-start = (f32[2,3,1024]{2,0,1:T(2,128)}, f32[2,3,1024]{2,0,1:T(2,128)S(1)}, u32[]{:S(2)}, u32[]{:S(2)}) collective-permute-start(f32[2,3,1024]{2,0,1:T(2,128)} %param.2), channel_id=1, source_target_pairs={{7,0},{0,1},{1,2},{2,3},{3,4},{4,5},{5,6},{6,7},{15,8},{8,9},{9,10... | collective-permute-start | bytes 73736 | tf_op jit(solution)/shard_map/ppermute | solution.py:22
  0.5 0.7 copy-start.29
  39.4 5.3 %collective-permute-start.1 = (f32[2,3,1024]{2,0,1:T(2,128)S(1)}, f32[2,3,1024]{2,0,1:T(2,128)S(1)}, u32[]{:S(2)}, u32[]{:S(2)}) collective-permute-start(f32[2,3,1024]{2,0,1:T(2,128)S(1)} %collective-permute-done), channel_id=1, source_target_pairs={{7,0},{0,1},{1,2},{2,3},{3,4},{4,5},{5,6},{6,7},{15,8},{8,9},{9,10... | collective-permute-start | bytes 73736 | tf_op jit(solution)/shard_map/ppermute | solution.py:22
  56.7 1.1 %copy-start.18 = (f32[2,1023]{0,1:T(8,128)S(1)}, f32[2,1023]{0,1:T(8,128)}, u32[]{:S(2)}) copy-start(f32[2,1023]{0,1:T(8,128)} %get-tuple-element.89) | copy-start | bytes 24556
  56.7 1.2 %copy-start.19 = (f32[2,1023]{0,1:T(8,128)S(1)}, f32[2,1023]{0,1:T(8,128)}, u32[]{:S(2)}) copy-start(f32[2,1023]{0,1:T(8,128)} %get-tuple-element.90) | copy-start | bytes 24556
  56.7 1.4 %copy-start.20 = (f32[2,1023]{0,1:T(8,128)S(1)}, f32[2,1023]{0,1:T(8,128)}, u32[]{:S(2)}) copy-start(f32[2,1023]{0,1:T(8,128)} %get-tuple-element.57) | copy-start | bytes 24556
  56.7 1.5 %copy-start.21 = (f32[2,1023]{0,1:T(8,128)S(1)}, f32[2,1023]{0,1:T(8,128)}, u32[]{:S(2)}) copy-start(f32[2,1023]{0,1:T(8,128)} %get-tuple-element.58) | copy-start | bytes 24556
  62.1 0.8 copy-start.2
  63.9 1.0 %copy-start.26 = (f32[2,992]{0,1:T(8,128)S(1)}, f32[2,992]{0,1:T(8,128)}, u32[]{:S(2)}) copy-start(f32[2,992]{0,1:T(8,128)} %get-tuple-element.55) | copy-start | bytes 23812
  63.9 1.2 %copy-start.27 = (f32[2,992]{0,1:T(8,128)S(1)}, f32[2,992]{0,1:T(8,128)}, u32[]{:S(2)}) copy-start(f32[2,992]{0,1:T(8,128)} %get-tuple-element.56) | copy-start | bytes 23812
  66.4 0.8 copy-start.4
  66.4 1.0 %copy-start.6 = (f32[2,1024]{0,1:T(8,128)}, f32[2,1024]{0,1:T(8,128)S(1)}, u32[]{:S(2)}) copy-start(f32[2,1024]{0,1:T(8,128)S(1)} %get-tuple-element.150) | copy-start | bytes 24580
  66.5 1.3 %copy-start.10 = (f32[2,1024]{0,1:T(8,128)S(1)}, f32[2,1024]{0,1:T(8,128)}, u32[]{:S(2)}) copy-start(f32[2,1024]{0,1:T(8,128)} %get-tuple-element.17) | copy-start | bytes 24580
  67.9 1.0 %copy-start.9 = (f32[2,1024]{0,1:T(8,128)S(1)}, f32[2,1024]{0,1:T(8,128)}, u32[]{:S(2)}) copy-start(f32[2,1024]{0,1:T(8,128)} %get-tuple-element.149) | copy-start | bytes 24580
  68.9 1.0 %copy-start.25 = (f32[2,1023]{0,1:T(8,128)S(1)}, f32[2,1023]{0,1:T(8,128)}, u32[]{:S(2)}) copy-start(f32[2,1023]{0,1:T(8,128)} %get-tuple-element.86) | copy-start | bytes 24556
  69.0 1.1 %copy-start.3 = (f32[2,1024]{0,1:T(8,128)S(1)}, f32[2,1024]{0,1:T(8,128)}, u32[]{:S(2)}) copy-start(f32[2,1024]{0,1:T(8,128)} %copy-done.2) | copy-start | bytes 24580
  69.0 1.3 %copy-start.5 = (f32[2,1024]{0,1:T(8,128)S(1)}, f32[2,1024]{0,1:T(8,128)}, u32[]{:S(2)}) copy-start(f32[2,1024]{0,1:T(8,128)} %copy-done.4) | copy-start | bytes 24580
  69.0 1.4 %copy-start.7 = (f32[2,1024]{0,1:T(8,128)S(1)}, f32[2,1024]{0,1:T(8,128)}, u32[]{:S(2)}) copy-start(f32[2,1024]{0,1:T(8,128)} %copy-done.6) | copy-start | bytes 24580
  69.0 1.6 %copy-start.24 = (f32[2,1023]{0,1:T(8,128)S(1)}, f32[2,1023]{0,1:T(8,128)}, u32[]{:S(2)}) copy-start(f32[2,1023]{0,1:T(8,128)} %get-tuple-element.85) | copy-start | bytes 24556
  76.8 0.8 copy-start.8
  77.5 1.1 %copy-start.16 = (f32[2,1023]{0,1:T(8,128)S(1)}, f32[2,1023]{0,1:T(8,128)}, u32[]{:S(2)}) copy-start(f32[2,1023]{0,1:T(8,128)} %get-tuple-element.41) | copy-start | bytes 24556
  77.5 1.2 %copy-start.17 = (f32[2,1023]{0,1:T(8,128)S(1)}, f32[2,1023]{0,1:T(8,128)}, u32[]{:S(2)}) copy-start(f32[2,1023]{0,1:T(8,128)} %get-tuple-element.42) | copy-start | bytes 24556
  77.6 1.4 %copy-start.22 = (f32[2,1023]{0,1:T(8,128)S(1)}, f32[2,1023]{0,1:T(8,128)}, u32[]{:S(2)}) copy-start(f32[2,1023]{0,1:T(8,128)} %get-tuple-element.77) | copy-start | bytes 24556
  77.6 1.5 %copy-start.23 = (f32[2,1023]{0,1:T(8,128)S(1)}, f32[2,1023]{0,1:T(8,128)}, u32[]{:S(2)}) copy-start(f32[2,1023]{0,1:T(8,128)} %get-tuple-element.78) | copy-start | bytes 24556
  86.4 1.1 %copy-start = (f32[2,1024]{0,1:T(8,128)}, f32[2,1024]{0,1:T(8,128)S(1)}, u32[]{:S(2)}) copy-start(f32[2,1024]{0,1:T(8,128)S(1)} %get-tuple-element.10) | copy-start | bytes 24580
  86.9 2.0 %copy-start.15 = (f32[2,1023]{0,1:T(8,128)S(1)}, f32[2,1023]{0,1:T(8,128)}, u32[]{:S(2)}) copy-start(f32[2,1023]{0,1:T(8,128)} %get-tuple-element.65) | copy-start | bytes 24556
  87.7 1.3 %copy-start.14 = (f32[2,1023]{0,1:T(8,128)S(1)}, f32[2,1023]{0,1:T(8,128)}, u32[]{:S(2)}) copy-start(f32[2,1023]{0,1:T(8,128)} %get-tuple-element.70) | copy-start | bytes 24556
  88.9 1.1 %copy-start.1 = (f32[2,1024]{0,1:T(8,128)S(1)}, f32[2,1024]{0,1:T(8,128)}, u32[]{:S(2)}) copy-start(f32[2,1024]{0,1:T(8,128)} %copy-done) | copy-start | bytes 24580
  88.9 1.2 %copy-start.11 = (f32[2,1023]{0,1:T(8,128)S(1)}, f32[2,1023]{0,1:T(8,128)}, u32[]{:S(2)}) copy-start(f32[2,1023]{0,1:T(8,128)} %get-tuple-element.33) | copy-start | bytes 24556
  88.9 1.4 %copy-start.12 = (f32[2,1023]{0,1:T(8,128)S(1)}, f32[2,1023]{0,1:T(8,128)}, u32[]{:S(2)}) copy-start(f32[2,1023]{0,1:T(8,128)} %get-tuple-element.34) | copy-start | bytes 24556
  88.9 1.5 %copy-start.13 = (f32[2,1023]{0,1:T(8,128)S(1)}, f32[2,1023]{0,1:T(8,128)}, u32[]{:S(2)}) copy-start(f32[2,1023]{0,1:T(8,128)} %get-tuple-element.69) | copy-start | bytes 24556
where the time goes:
time: 96.7 us; the launch traced here: 96.1 us
  local copies, waits for them, and re-layouts  35.6 us (37%)
  matrix products  18.5 us (19%)
  blocking collectives  18 us (19%)
  other arithmetic  16.4 us (17%)
  waiting for transfers between devices  4.96 us (5%)
  between operations  1.97 us (2%)
    dot_general x2, matrix products, pair_kernel(): jnp.einsum('acp,bcp->abp', row_pictures, col_pictures, precision=lax.Prec...  18.5 us
    psum x1, blocking collectives, from_root(): return lax.psum(kept, axis)  18 us
    slice x24, local copies, waits for them, and re-layouts, box_sum(): from_left = jnp.concatenate([single, maps[..., :-1]], axis=-1)  11.6 us
    add x11, other arithmetic, box_sum(): maps + jnp.where(positions > 0, from_left, 0.0)  10.1 us
    unnamed x62, local copies, waits for them, and re-layouts  10 us
    ppermute x2, waiting for transfers between devices, passed_along(): return lax.ppermute(block, axis, route)  4.96 us
    dot_general x2, local copies, waits for them, and re-layouts, pair_kernel(): jnp.einsum('acp,bcp->abp', row_pictures, col_pictures, precision=lax.Prec...  2.84 us
    slice x24, local copies, waits for them, and re-layouts, box_sum(): from_above = jnp.concatenate([band, across[..., :-WIDTH]], axis=-1)  2.71 us
  transfers between devices with their start and end apart: 2, of which 1 were waited for; matrix products, arithmetic and copies ran while one was open for 5% of the time, Pallas kernels for 0%

commit v1 on v0

--- a/solution.py
+++ b/solution.py
@@ -13,7 +13,7 @@
 
 def from_root(value, axis, source):
     kept = jnp.where(lax.axis_index(axis) == source, value, 0).astype(value.dtype)
-    return lax.psum(kept, axis)
+    return jnp.sum(lax.all_gather(kept, axis), axis=0)
 
 
 def passed_along(block, axis, distance):

time: 96.7 us -> 55.4 us (0.57)
  local copies, waits for them, and re-layouts: 35.6 us -> 8.92 us
  other arithmetic: 16.4 us -> 5.74 us
  matrix products: 18.5 us -> 15.3 us
    all_gather x0 -> x2, blocking collectives: none -> 18.1 us  [from_root(): return jnp.sum(lax.all_gather(kept, axis), axis=0)]
    psum x1 -> x0, blocking collectives: 18 us -> none  [from_root(): return lax.psum(kept, axis)]
    slice x24, local copies, waits for them, and re-layouts: 11.6 us -> 1.85 us  [box_sum(): from_left = jnp.concatenate([single, maps[..., :-1]], axis=-1)]
    unnamed x62 -> x4, local copies, waits for them, and re-layouts: 10 us -> 0.68 us
    add x11 -> x13, other arithmetic: 10.1 us -> 1.26 us  [box_sum(): maps + jnp.where(positions > 0, from_left, 0.0)]
    dot_general x2, matrix products: 18.5 us -> 15.3 us  [pair_kernel(): jnp.einsum('acp,bcp->abp', row_pictures, col_pictures, precision=lax.Prec...]
    add x16 -> x0, local copies, waits for them, and re-layouts: 2.96 us -> none  [the longest x12 2.2 us: self_maps(): level = weight_var / 9.0 * box_sum(0.5 * level) + bias_var]
    dot_general x2, local copies, waits for them, and re-layouts: 2.84 us -> 0.94 us  [pair_kernel(): jnp.einsum('acp,bcp->abp', row_pictures, col_pictures, precision=lax.Prec...]
  transfers between devices with their start and end apart: 2 -> 2, of which waited for: 1 -> 1; matrix products, arithmetic and copies ran while one was open for 5% -> 4% of each run, Pallas kernels for 0% -> 0%
where the time goes in v1:
time: 55.4 us; the launch traced here: 55.2 us
  blocking collectives  18.1 us (33%)
  matrix products  15.3 us (28%)
  local copies, waits for them, and re-layouts  8.92 us (16%)
  other arithmetic  5.74 us (10%)
  waiting for transfers between devices  4.96 us (9%)
  between operations  1.58 us (3%)
  starting transfers between devices  0.64 us (1%)
    all_gather x2, blocking collectives, from_root(): return jnp.sum(lax.all_gather(kept, axis), axis=0)  18.1 us
    dot_general x2, matrix products, pair_kernel(): jnp.einsum('acp,bcp->abp', row_pictures, col_pictures, precision=lax.Prec...  15.3 us
    ppermute x2, waiting for transfers between devices, passed_along(): return lax.ppermute(block, axis, route)  4.96 us
    ppermute x2, local copies, waits for them, and re-layouts, passed_along(): return lax.ppermute(block, axis, route)  1.87 us
    slice x24, local copies, waits for them, and re-layouts, box_sum(): from_left = jnp.concatenate([single, maps[..., :-1]], axis=-1)  1.85 us
    slice x24, local copies, waits for them, and re-layouts, box_sum(): from_above = jnp.concatenate([band, across[..., :-WIDTH]], axis=-1)  1.85 us
    div x6, other arithmetic, relu_map(): scale_ab * (jnp.sqrt(1.0 - cosine * cosine) + (math.pi - jnp.arccos(cosin...  1.61 us
    add x13, other arithmetic, box_sum(): maps + jnp.where(positions > 0, from_left, 0.0)  1.26 us
  transfers between devices with their start and end apart: 2, of which 1 were waited for; matrix products, arithmetic and copies ran while one was open for 4% of the time, Pallas kernels for 0%

profile of v1, /device:TPU:0, one launch (start us, length us, event | category | flops | bytes accessed | tf_op | source)
XLA Modules:
  0.0 55.2 jit_solution(16238779924178846801)
XLA Ops:
  0.0 0.5 collective-permute-start
  0.5 0.7 %copy-done.1 = s32[2,8]{1,0:T(2,128)S(1)} copy-done((s32[2,8]{1,0:T(2,128)S(1)}, s32[2,8]{1,0:T(2,128)}, u32[]{:S(2)}) %copy-start.1) | copy-done | bytes 88
  1.1 0.6 %constant_dynamic-slice_fusion.1 = (s32[1,1]{1,0:T(1,128)}, s32[1,1]{1,0:T(1,128)}) fusion(s32[2,8]{1,0:T(2,128)S(1)} %copy-done.1, s32[]{:T(128)S(6)} %select_n.313), kind=kLoop, calls=%fused_computation.81 | loop fusion | bytes 20 | tf_op jit(solution)/shard_map/dynamic_slice | solution.py:81
  3.1 9.7 %all-gather = f32[8,3,1024]{2,1,0:T(4,128)S(1)} all-gather(f32[2,3,1024]{2,1,0:T(4,128)S(1)} %get-tuple-element.32), channel_id=2, replica_groups=mesh['row'=4,'col'=8] {'row'}, dimensions={0}, use_global_device_ids=true | all-gather | bytes 122880 | tf_op jit(solution)/shard_map/all_gather | solution.py:16
  12.9 8.4 %all-gather.1 = f32[8,3,1024]{2,1,0:T(4,128)S(1)} all-gather(f32[2,3,1024]{2,1,0:T(4,128)S(1)} %get-tuple-element.33), channel_id=3, replica_groups=mesh['row'=4,'col'=8] {'row'}, dimensions={0}, use_global_device_ids=true | all-gather | bytes 122880 | tf_op jit(solution)/shard_map/all_gather | solution.py:16
  21.6 0.1 broadcast_multiply_fusion.11
  21.8 0.6 copy.38
  22.4 0.6 %copy.43 = f32[2,3,1024]{1,0,2:T(2,128)S(1)} copy(f32[2,3,1024]{2,1,0:T(4,128)S(1)} %reduce_sum.76) | data formatting | bytes 49152 | tf_op jit(solution)/shard_map/reduce_sum | solution.py:16
  23.0 1.3 %copy.39 = f32[2,3,1024]{1,0,2:T(2,128)} copy(f32[2,3,1024]{2,0,1:T(2,128)S(1)} %collective-permute-done) | data formatting | bytes 49152 | tf_op jit(solution)/shard_map/ppermute | solution.py:22
  24.3 8.2 %fusion.54 = f32[1024,2,2]{2,1,0:T(2,128)S(1)} fusion(f32[2,3,1024]{1,0,2:T(2,128)S(1)} %copy.38, f32[2,3,1024]{1,0,2:T(2,128)} %copy.39), kind=kOutput, calls=%fused_computation.130 | convolution fusion | flops 147456 | bytes 65536 | tf_op jit(solution)/shard_map/acp,bcp->abp/dot_general | solution.py:63
  32.4 0.5 copy.40
  32.9 0.1 fusion.13
  33.0 0.1 select_add_fusion.7
  33.3 0.1 select_add_fusion.19
  33.5 0.3 multiply_multiply_fusion.5
  33.9 0.1 select_add_fusion.6
  34.1 0.1 broadcast_multiply_fusion.5
  34.3 0.2 collective-permute-start.1
  34.6 5.0 %collective-permute-done.1 = f32[2,3,1024]{2,0,1:T(2,128)S(1)} collective-permute-done((f32[2,3,1024]{2,0,1:T(2,128)S(1)}, f32[2,3,1024]{2,0,1:T(2,128)S(1)}, u32[]{:S(2)}, u32[]{:S(2)}) %collective-permute-start.1) | collective-permute-done | bytes 24608 | tf_op jit(solution)/shard_map/ppermute | solution.py:22
  39.6 0.1 select_add_fusion.22
  39.9 0.1 broadcast_multiply_fusion.7
  40.1 0.3 multiply_multiply_fusion.4
  40.4 0.1 select_add_fusion.5
  40.8 0.1 broadcast_multiply_fusion.2
  41.0 0.1 broadcast_multiply_fusion.4
  41.3 0.1 select_add_fusion.21
  41.5 0.1 broadcast_multiply_fusion.6
  41.7 0.3 multiply_multiply_fusion.3
  42.1 0.6 %copy.44 = f32[2,3,1024]{1,0,2:T(2,128)S(1)} copy(f32[2,3,1024]{2,0,1:T(2,128)S(1)} %collective-permute-done.1) | data formatting | bytes 49152 | tf_op jit(solution)/shard_map/ppermute | solution.py:22
  42.6 7.1 %fusion.55 = f32[1024,2,2]{2,1,0:T(2,128)S(1)} fusion(f32[2,3,1024]{1,0,2:T(2,128)S(1)} %copy.43, f32[2,3,1024]{1,0,2:T(2,128)S(1)} %copy.44), kind=kOutput, calls=%fused_computation.131 | convolution fusion | flops 147456 | bytes 65536 | tf_op jit(solution)/shard_map/acp,bcp->abp/dot_general | solution.py:63
  49.8 0.5 copy.45
  50.2 0.1 fusion.21
  50.3 0.1 select_add_fusion.4
  50.5 0.3 multiply_multiply_fusion.2
  50.9 0.1 select_add_fusion.2
  51.1 0.1 broadcast_multiply_fusion.1
  51.2 0.3 multiply_multiply_fusion.1
  51.6 0.1 select_add_fusion.1
  52.0 0.1 broadcast_multiply_fusion.3
  52.2 0.1 select_add_fusion.20
  52.5 0.3 multiply_multiply_fusion
  52.9 0.1 select_add_fusion
  53.1 0.1 select_add_fusion.8
  53.3 0.1 multiply_add_fusion
  53.5 0.3 multiply_reduce_fusion.2
  54.1 0.1 multiply_add_fusion.8
  54.3 0.3 multiply_reduce_fusion.3
  54.6 0.6 %pad_maximum_fusion = f32[2,2,2]{2,1,0:T(2,128)} fusion(f32[1,2,2]{2,1,0:T(2,128)S(1)} %add_bitcast_fusion, f32[1,2,2]{2,1,0:T(2,128)S(1)} %add_bitcast_fusion.1), kind=kLoop, calls=%fused_computation.77 | loop fusion | flops 8 | bytes 64 | tf_op jit(solution)/shard_map/stack | solution.py:87
  (68 shorter events, 4.3 us)
Async XLA Ops:
  0.0 3.0 %copy-start = (f32[2,3,1024]{2,0,1:T(2,128)S(1)}, f32[2,3,1024]{2,0,1:T(2,128)}, u32[]{:S(2)}) copy-start(f32[2,3,1024]{2,0,1:T(2,128)} %param.2) | copy-start | bytes 73732
  0.0 22.9 %collective-permute-start = (f32[2,3,1024]{2,0,1:T(2,128)}, f32[2,3,1024]{2,0,1:T(2,128)S(1)}, u32[]{:S(2)}, u32[]{:S(2)}) collective-permute-start(f32[2,3,1024]{2,0,1:T(2,128)} %param.2), channel_id=1, source_target_pairs={{7,0},{0,1},{1,2},{2,3},{3,4},{4,5},{5,6},{6,7},{15,8},{8,9},{9,10... | collective-permute-start | bytes 73736 | tf_op jit(solution)/shard_map/ppermute | solution.py:22
  0.5 0.7 %copy-start.1 = (s32[2,8]{1,0:T(2,128)S(1)}, s32[2,8]{1,0:T(2,128)}, u32[]{:S(2)}) copy-start(s32[2,8]{1,0:T(2,128)} %param.3) | copy-start | bytes 196
  34.3 5.2 %collective-permute-start.1 = (f32[2,3,1024]{2,0,1:T(2,128)S(1)}, f32[2,3,1024]{2,0,1:T(2,128)S(1)}, u32[]{:S(2)}, u32[]{:S(2)}) collective-permute-start(f32[2,3,1024]{2,0,1:T(2,128)S(1)} %collective-permute-done), channel_id=1, source_target_pairs={{7,0},{0,1},{1,2},{2,3},{3,4},{4,5},{5,6},{6,7},{15,8},{8,9},{9,10... | collective-permute-start | bytes 73736 | tf_op jit(solution)/shard_map/ppermute | solution.py:22
